TPU v7x, 32 devices: a whole 2x2x4 slice. The times are simulated.
32 devices in a mesh: row: 8 (over z, x), col: 4 (over y, core).
Axes of the slice: x: 2, y: 2, z: 4, core: 2. Of those that a mesh axis runs over, the one named last changes fastest.
Arguments:
- slab: float32 [4096, 4096], P('row', 'col'), may hold values from -32 to 32, as said below
Outputs:
- factored: float32 [4096, 4096], P('row', 'col')
Inputs may be any that keep to these rules, and one draw needn't show every extreme that they name: The slab holds the first 4096 columns of a symmetric positive definite matrix of order 4096, column blocks of 256 in the stored order of the first step.
All inputs are finite; a program needn't handle non-finite values.
Results may differ from a plain program's by a relative error of at most 0.00029.
Values sent between devices are 32-bit elements; how exact they have to be, the bound alone decides.
No kernel may reach another device: no remote copies, remote signals or barrier semaphores. Data moves between devices by JAX's collectives and lax.ppermute only.
A program may use at most 128 MiB of HBM per device.

v0:
```python
import jax
import jax.numpy as jnp
from jax import lax
from jax.sharding import PartitionSpec as P

BLOCK = 256
PANELS = 2


PRECISE = lax.Precision.HIGHEST


def from_root(value, axis, source):
    kept = jnp.where(lax.axis_index(axis) == source, value, 0).astype(value.dtype)
    return lax.psum(kept, axis)


def product(left_side, right_side):
    return jnp.dot(left_side, right_side, precision=PRECISE, preferred_element_type=jnp.float32)


def shards(slab):
    row_count, local_width = slab.shape
    col_count = lax.axis_size("col")
    row_index = lax.axis_index("row")
    col_index = lax.axis_index("col")
    blocks_here = local_width // BLOCK
    row_ids = row_index * row_count + jnp.arange(row_count, dtype=jnp.int32)
    global_ids = jnp.arange(blocks_here, dtype=jnp.int32) * col_count + col_index
    identity = jnp.eye(BLOCK, dtype=jnp.float32)
    state = slab
    previous = None
    for sub_step in range(2 * PANELS):
        start = sub_step * BLOCK
        stop = start + BLOCK
        owner_col = sub_step % col_count
        local_block = sub_step // col_count
        home_row = start // row_count
        offset = start % row_count
        first_col = local_block * BLOCK
        column_old = state[:, first_col : first_col + BLOCK]
        diag_tile = column_old[offset : offset + BLOCK]
        if sub_step % 2 == 1:
            cross_tile = previous[offset : offset + BLOCK]
        else:
            cross_tile = jnp.zeros((BLOCK, BLOCK), jnp.float32)
        diag_tile, cross_tile = (
            from_root(diag_tile, "row", home_row),
            from_root(cross_tile, "row", home_row),
        )
        column = column_old
        if sub_step % 2 == 1:
            diag_tile = diag_tile - product(cross_tile, cross_tile.T)
            column = column - product(previous, cross_tile.T)
        lower_factor = jnp.linalg.cholesky(diag_tile)
        inverse = jax.scipy.linalg.solve_triangular(lower_factor, identity, lower=True)
        factor = product(column, inverse.T)
        factor = jnp.where(row_ids[:, None] < start, jnp.float32(0.0), factor)
        factor = factor.at[offset : offset + BLOCK].set(
            jnp.where(row_index == home_row, lower_factor, factor[offset : offset + BLOCK])
        )
        state = state.at[:, first_col : first_col + BLOCK].set(
            jnp.where(col_index == owner_col, factor, column_old)
        )
        column_piece = from_root(factor, "col", owner_col)
        if sub_step % 2 == 1:
            panel_left = jnp.concatenate([previous, column_piece], axis=1)
            fetched_list = []
            for column_slot in range(blocks_here):
                first_row = (column_slot * col_count + col_index) * BLOCK
                source_row = first_row // row_count
                within = first_row % row_count
                rows_part = lax.dynamic_slice_in_dim(panel_left, within, BLOCK, 0)
                fetched_list.append(from_root(rows_part, "row", source_row))
            mirrored = jnp.stack(fetched_list, axis=0)
            blocks = state.reshape(row_count, blocks_here, BLOCK)
            change = jnp.einsum("rp,kcp->rkc", panel_left, mirrored, precision=PRECISE)
            keep_mask = (row_ids[:, None, None] >= stop) & (global_ids[None, :, None] > sub_step)
            blocks = jnp.where(keep_mask, blocks - change, blocks)
            state = blocks.reshape(row_count, local_width)
        previous = column_piece
    return state


def solution(mesh):
    in_specs = (P("row", "col"),)
    out_specs = P("row", "col")
    return jax.shard_map(shards, mesh=mesh, in_specs=in_specs, out_specs=out_specs, check_vma=False)
```

profile of v0, /device:TPU:14, one launch (start us, length us, event | category | flops | bytes accessed | tf_op | source)
XLA Modules:
  0.0 971.1 jit_solution(18297693542058628579)
XLA Ops:
  10.1 71.8 %all-reduce.16.cloned.1.call-done = f32[256,256]{0,1:T(8,128)} async-done(((f32[256,256]{0,1:T(8,128)}), f32[256,256]{0,1:T(8,128)}) %all-reduce.16.cloned.1.call-update) | async-done | bytes 262160 | tf_op jit(solution)/shard_map/psum | solution.py:15
  84.0 11.7 %cholesky.214 = f32[128,128]{1,0:T(8,128)S(1)} custom-call(f32[128,128]{1,0:T(8,128)S(1)} %cholesky.346), custom_call_target="Cholesky" | custom-call | tf_op jit(solution)/shard_map/jit(cholesky)/cholesky | solution.py:55
  95.8 9.8 %custom-call.17 = f32[1,128,128]{1,2,0:T(8,128)S(1)} custom-call(f32[1,128,128]{2,1,0:T(8,128)S(1)} %get-tuple-element.225), custom_call_target="InvertDiagBlocksLowerTriangular" | custom-call | tf_op jit(solution)/shard_map/jit(cholesky)/cholesky | solution.py:55
  108.0 11.7 %cholesky.231 = f32[128,128]{1,0:T(8,128)S(1)} custom-call(f32[128,128]{1,0:T(8,128)S(1)} %convolution_subtract_fusion.11), custom_call_target="Cholesky" | custom-call | tf_op jit(solution)/shard_map/jit(cholesky)/cholesky | solution.py:55
  122.7 6.1 while.16
  128.8 19.9 %custom-call.18 = f32[2,128,128]{1,2,0:T(8,128)S(1)} custom-call(f32[2,128,128]{2,1,0:T(8,128)S(1)} %get-tuple-element.129), custom_call_target="InvertDiagBlocksLowerTriangular" | custom-call | tf_op jit(solution)/shard_map/jit(_solve_triangular)/triangular_solve | solution.py:56
  153.6 31.2 %all-reduce.18.cloned.1.call-done = f32[512,256]{0,1:T(8,128)} async-done(((f32[512,256]{0,1:T(8,128)}), f32[512,256]{0,1:T(8,128)}) %all-reduce.18.cloned.1.call-update) | async-done | bytes 524304 | tf_op jit(solution)/shard_map/psum | solution.py:15
  186.6 75.2 %all-reduce.34.cloned.1.call-done = (f32[256,256]{0,1:T(8,128)}, f32[256,256]{0,1:T(8,128)}) async-done(((f32[256,256]{0,1:T(8,128)}, f32[256,256]{0,1:T(8,128)}), (f32[256,256]{0,1:T(8,128)}, f32[256,256]{0,1:T(8,128)})) %all-reduce.34.cloned.1.call-update) | async-done | bytes 524304 | tf_op jit(solution)/shard_map/psum | solution.py:15
  264.5 11.7 %cholesky.248 = f32[128,128]{1,0:T(8,128)S(1)} custom-call(f32[128,128]{1,0:T(8,128)S(1)} %cholesky.349), custom_call_target="Cholesky" | custom-call | tf_op jit(solution)/shard_map/jit(cholesky)/cholesky | solution.py:55
  276.3 9.8 %custom-call.19 = f32[1,128,128]{1,2,0:T(8,128)S(1)} custom-call(f32[1,128,128]{2,1,0:T(8,128)S(1)} %get-tuple-element.223), custom_call_target="InvertDiagBlocksLowerTriangular" | custom-call | tf_op jit(solution)/shard_map/jit(cholesky)/cholesky | solution.py:55
  289.7 11.7 %cholesky.265 = f32[128,128]{1,0:T(8,128)S(1)} custom-call(f32[128,128]{1,0:T(8,128)S(1)} %convolution_subtract_fusion.10), custom_call_target="Cholesky" | custom-call | tf_op jit(solution)/shard_map/jit(cholesky)/cholesky | solution.py:55
  306.2 7.7 while.17
  313.9 21.1 %custom-call.20 = f32[2,128,128]{1,2,0:T(8,128)} custom-call(f32[2,128,128]{2,1,0:T(8,128)} %get-tuple-element.130), custom_call_target="InvertDiagBlocksLowerTriangular" | custom-call | tf_op jit(solution)/shard_map/jit(_solve_triangular)/triangular_solve | solution.py:56
  343.8 30.9 %all-reduce.20.cloned.1.call-done = f32[512,256]{0,1:T(8,128)} async-done(((f32[512,256]{0,1:T(8,128)}), f32[512,256]{0,1:T(8,128)}) %all-reduce.20.cloned.1.call-update) | async-done | bytes 524304 | tf_op jit(solution)/shard_map/psum | solution.py:15
  385.5 97.0 %all-reduce.32.cloned.1.call-done = (f32[1,256,512]{1,2,0:T(8,128)}, f32[1,256,512]{1,2,0:T(8,128)}, f32[1,256,512]{1,2,0:T(8,128)}, f32[1,256,512]{1,2,0:T(8,128)}) async-done(((f32[1,256,512]{1,2,0:T(8,128)}, f32[1,256,512]{1,2,0:T(8,128)}, f32[1,256,512]{1,2,0:T(8,128)}, f32[1,256,512]{1,2,0:T(8,128)}), (f32[1,256,512]{1,2,0:T(8,128)}, f32[1,256,512]{1,2,0:T(8,128)}, f32[1,256,512]{1,2,0:T(8,128)}, ...) | async-done | bytes 2097168 | tf_op jit(solution)/shard_map/psum | solution.py:15
  482.5 5.7 subtract_select_fusion.1
  489.2 69.9 %all-reduce.22.cloned.1.call-done = f32[256,256]{0,1:T(8,128)} async-done(((f32[256,256]{0,1:T(8,128)}), f32[256,256]{0,1:T(8,128)}) %all-reduce.22.cloned.1.call-update) | async-done | bytes 262160 | tf_op jit(solution)/shard_map/psum | solution.py:15
  561.1 11.7 %cholesky.282 = f32[128,128]{1,0:T(8,128)S(1)} custom-call(f32[128,128]{1,0:T(8,128)S(1)} %cholesky.352), custom_call_target="Cholesky" | custom-call | tf_op jit(solution)/shard_map/jit(cholesky)/cholesky | solution.py:55
  573.0 9.8 %custom-call.21 = f32[1,128,128]{1,2,0:T(8,128)S(1)} custom-call(f32[1,128,128]{2,1,0:T(8,128)S(1)} %get-tuple-element.221), custom_call_target="InvertDiagBlocksLowerTriangular" | custom-call | tf_op jit(solution)/shard_map/jit(cholesky)/cholesky | solution.py:55
  583.4 11.7 %cholesky.299 = f32[128,128]{1,0:T(8,128)S(1)} custom-call(f32[128,128]{1,0:T(8,128)S(1)} %convolution_subtract_fusion.9), custom_call_target="Cholesky" | custom-call | tf_op jit(solution)/shard_map/jit(cholesky)/cholesky | solution.py:55
  598.0 4.3 while.18
  602.4 19.7 %custom-call.22 = f32[2,128,128]{1,2,0:T(8,128)S(1)} custom-call(f32[2,128,128]{2,1,0:T(8,128)S(1)} %get-tuple-element.131), custom_call_target="InvertDiagBlocksLowerTriangular" | custom-call | tf_op jit(solution)/shard_map/jit(_solve_triangular)/triangular_solve | solution.py:56
  626.2 31.4 %all-reduce.24.cloned.1.call-done = f32[512,256]{0,1:T(8,128)} async-done(((f32[512,256]{0,1:T(8,128)}), f32[512,256]{0,1:T(8,128)}) %all-reduce.24.cloned.1.call-update) | async-done | bytes 524304 | tf_op jit(solution)/shard_map/psum | solution.py:15
  659.6 75.0 %all-reduce.30.cloned.1.call-done = (f32[256,256]{0,1:T(8,128)}, f32[256,256]{0,1:T(8,128)}) async-done(((f32[256,256]{0,1:T(8,128)}, f32[256,256]{0,1:T(8,128)}), (f32[256,256]{0,1:T(8,128)}, f32[256,256]{0,1:T(8,128)})) %all-reduce.30.cloned.1.call-update) | async-done | bytes 524304 | tf_op jit(solution)/shard_map/psum | solution.py:15
  737.2 11.7 %cholesky.316 = f32[128,128]{1,0:T(8,128)S(1)} custom-call(f32[128,128]{1,0:T(8,128)S(1)} %cholesky.355), custom_call_target="Cholesky" | custom-call | tf_op jit(solution)/shard_map/jit(cholesky)/cholesky | solution.py:55
  749.0 9.8 %custom-call.23 = f32[1,128,128]{1,2,0:T(8,128)S(1)} custom-call(f32[1,128,128]{2,1,0:T(8,128)S(1)} %get-tuple-element.219), custom_call_target="InvertDiagBlocksLowerTriangular" | custom-call | tf_op jit(solution)/shard_map/jit(cholesky)/cholesky | solution.py:55
  762.4 11.7 %cholesky.333 = f32[128,128]{1,0:T(8,128)S(1)} custom-call(f32[128,128]{1,0:T(8,128)S(1)} %convolution_subtract_fusion.8), custom_call_target="Cholesky" | custom-call | tf_op jit(solution)/shard_map/jit(cholesky)/cholesky | solution.py:55
  778.8 7.4 while.19
  786.2 21.1 %custom-call.24 = f32[2,128,128]{1,2,0:T(8,128)} custom-call(f32[2,128,128]{2,1,0:T(8,128)} %get-tuple-element.132), custom_call_target="InvertDiagBlocksLowerTriangular" | custom-call | tf_op jit(solution)/shard_map/jit(_solve_triangular)/triangular_solve | solution.py:56
  815.9 31.0 %all-reduce.26.cloned.1.call-done = f32[512,256]{0,1:T(8,128)} async-done(((f32[512,256]{0,1:T(8,128)}), f32[512,256]{0,1:T(8,128)}) %all-reduce.26.cloned.1.call-update) | async-done | bytes 524304 | tf_op jit(solution)/shard_map/psum | solution.py:15
  849.5 105.1 %all-reduce.28.cloned.1.call-done = (f32[1,256,512]{1,2,0:T(8,128)}, f32[1,256,512]{1,2,0:T(8,128)}, f32[1,256,512]{1,2,0:T(8,128)}, f32[1,256,512]{1,2,0:T(8,128)}) async-done(((f32[1,256,512]{1,2,0:T(8,128)}, f32[1,256,512]{1,2,0:T(8,128)}, f32[1,256,512]{1,2,0:T(8,128)}, f32[1,256,512]{1,2,0:T(8,128)}), (f32[1,256,512]{1,2,0:T(8,128)}, f32[1,256,512]{1,2,0:T(8,128)}, f32[1,256,512]{1,2,0:T(8,128)}, ...) | async-done | bytes 2097168 | tf_op jit(solution)/shard_map/psum | solution.py:15
  954.6 6.4 subtract_select_fusion
  (196 shorter events, 105.1 us)
Async XLA Ops:
  6.5 75.3 %all-reduce.16.cloned.1.call-start = ((), (), s32[]{:S(2)}) async-start(), calls=%async_computation | async-start | bytes 524288 | tf_op jit(solution)/shard_map/psum | solution.py:15
  9.0 175.8 %all-reduce.18.cloned.1.call-start = ((), (), s32[]{:S(2)}) async-start(), calls=%async_computation.1 | async-start | bytes 1048576 | tf_op jit(solution)/shard_map/psum | solution.py:15
  84.0 11.9 %copy-start.3 = (f32[256,256]{1,0:T(8,128)}, f32[256,256]{1,0:T(8,128)S(1)}, u32[]{:S(2)}) copy-start(f32[256,256]{1,0:T(8,128)S(1)} %fusion.44) | copy-start | bytes 786436
  152.7 188.1 %copy-start = (f32[512,256]{0,1:T(8,128)}, f32[512,256]{0,1:T(8,128)S(1)}, u32[]{:S(2)}) copy-start(f32[512,256]{0,1:T(8,128)S(1)} %get-tuple-element.217) | copy-start | bytes 1572868
  152.7 109.1 %all-reduce.34.cloned.1.call-start = ((), (), s32[]{:S(2)}) async-start(), calls=%async_computation.9 | async-start | bytes 1048576 | tf_op jit(solution)/shard_map/psum | solution.py:15
  186.6 188.1 %all-reduce.20.cloned.1.call-start = ((), (), s32[]{:S(2)}) async-start(), calls=%async_computation.2 | async-start | bytes 1048576 | tf_op jit(solution)/shard_map/psum | solution.py:15
  263.7 0.7 copy-start.4
  301.5 36.9 %copy-start.1 = (f32[512,256]{0,1:T(8,128)S(1)}, f32[512,256]{0,1:T(8,128)}, u32[]{:S(2)}) copy-start(f32[512,256]{0,1:T(8,128)} %all-reduce.18.cloned.1.call-done) | copy-start | bytes 1572868
  342.6 139.8 %all-reduce.32.cloned.1.call-start = ((), (), s32[]{:S(2)}) async-start(), calls=%async_computation.8 | async-start | bytes 4194304 | tf_op jit(solution)/shard_map/psum | solution.py:15
  377.2 181.8 %all-reduce.22.cloned.1.call-start = ((), (), s32[]{:S(2)}) async-start(), calls=%async_computation.3 | async-start | bytes 524288 | tf_op jit(solution)/shard_map/psum | solution.py:15
  489.0 168.6 %all-reduce.24.cloned.1.call-start = ((), (), s32[]{:S(2)}) async-start(), calls=%async_computation.4 | async-start | bytes 1048576 | tf_op jit(solution)/shard_map/psum | solution.py:15
  625.4 109.1 %all-reduce.30.cloned.1.call-start = ((), (), s32[]{:S(2)}) async-start(), calls=%async_computation.7 | async-start | bytes 1048576 | tf_op jit(solution)/shard_map/psum | solution.py:15
  659.3 187.6 %all-reduce.26.cloned.1.call-start = ((), (), s32[]{:S(2)}) async-start(), calls=%async_computation.5 | async-start | bytes 1048576 | tf_op jit(solution)/shard_map/psum | solution.py:15
  736.5 0.7 copy-start.5
  774.3 36.5 %copy-start.2 = (f32[512,256]{0,1:T(8,128)S(1)}, f32[512,256]{0,1:T(8,128)}, u32[]{:S(2)}) copy-start(f32[512,256]{0,1:T(8,128)} %all-reduce.24.cloned.1.call-done) | copy-start | bytes 1572868
  814.8 139.9 %all-reduce.28.cloned.1.call-start = ((), (), s32[]{:S(2)}) async-start(), calls=%async_computation.6 | async-start | bytes 4194304 | tf_op jit(solution)/shard_map/psum | solution.py:15
Sparse Core Ops, SparseCore 0:
  10.7 71.1 all-reduce.15
  152.9 31.9 all-reduce.17
  188.7 73.0 all-reduce.33
  342.7 31.9 all-reduce.19
  378.5 103.8 all-reduce.31
  489.1 69.9 all-reduce.21
  625.6 31.9 all-reduce.23
  661.4 73.0 all-reduce.29
  814.9 31.9 all-reduce.25
  850.7 103.8 all-reduce.27
where the time goes:
time: 984 us; the launch traced here: 971 us
  waiting for transfers between devices  619 us (63%)
  other arithmetic  241 us (24%)
  local copies, waits for them, and re-layouts  50.6 us (5%)
  matrix products  39.4 us (4%)
  between operations  19.9 us (2%)
    psum x10, waiting for transfers between devices, from_root(): return lax.psum(kept, axis)  618 us
    another operation x27, other arithmetic, shards(): lower_factor = jnp.linalg.cholesky(diag_tile)  138 us
    another operation x9, other arithmetic, shards(): jax.scipy.linalg.solve_triangular(lower_factor, identity, lower=True)  84 us
    another operation x45, local copies, waits for them, and re-layouts, shards(): jax.scipy.linalg.solve_triangular(lower_factor, identity, lower=True)  26 us
  transfers between devices with their start and end apart: 10, of which 10 were waited for; matrix products, arithmetic and copies ran while one was open for 1% of the time, Pallas kernels for 0%

commit v1 on v0

v1 whole, which is shorter than its diff:
```python
import functools

import jax
import jax.numpy as jnp
from jax import lax
from jax.experimental import pallas as pl
from jax.experimental.pallas import tpu as pltpu
from jax.sharding import PartitionSpec as P

BLOCK = 256
PANELS = 2
LEAF = 128
SUB = 8
HEAD_BLOCKS = 2 * PANELS
HEAD = HEAD_BLOCKS * BLOCK
NT = (((1,), (1,)), ((), ()))
NN = (((1,), (0,)), ((), ()))


def exact(left_side, right_side, dims=NT):
    return lax.dot_general(left_side, right_side, dims, precision=lax.Precision.HIGHEST, preferred_element_type=jnp.float32)


def split(value):
    high = value.astype(jnp.bfloat16)
    low = (value - high.astype(jnp.float32)).astype(jnp.bfloat16)
    return high, low


def three(left_side, right_side):
    def dot(a, b):
        return lax.dot_general(a, b, NT, preferred_element_type=jnp.float32)
    return dot(left_side[0], right_side[1]) + dot(left_side[1], right_side[0]) + dot(left_side[0], right_side[0])


def lane(value, index):
    return jnp.broadcast_to(value[:, index : index + 1], (SUB, LEAF))


def sublane(value, index):
    return jnp.broadcast_to(value[index : index + 1, :], (SUB, LEAF))


def leaf(block):
    groups = LEAF // SUB
    rows = lax.broadcasted_iota(jnp.int32, (SUB, LEAF), 0)
    cols = lax.broadcasted_iota(jnp.int32, (SUB, LEAF), 1)
    left = [block[SUB * g : SUB * g + SUB, :] for g in range(groups)]
    right = [jnp.where(cols == rows + SUB * g, 1.0, 0.0).astype(jnp.float32) for g in range(groups)]
    upper, inverse = [], []
    for p in range(groups):
        columns = [lane(left[p], SUB * p + j) for j in range(SUB)]
        here_left, here_right = left[p], right[p]
        pivots, rows_left, rows_right, heads = [], [], [], []
        scale = jnp.zeros((SUB, LEAF), jnp.float32)
        for j in range(SUB):
            root = lax.rsqrt(sublane(columns[j], j))
            pivot = root * root
            scale = jnp.where(rows == j, root, scale)
            factor = jnp.where(rows > j, columns[j] * pivot, 0.0)
            row_left, row_right = sublane(here_left, j), sublane(here_right, j)
            head = {l: sublane(columns[l], j) for l in range(j + 1, SUB)}
            for l in range(j + 1, SUB):
                columns[l] = columns[l] - factor * head[l]
            here_left = here_left - factor * row_left
            here_right = here_right - factor * row_right
            pivots.append(pivot)
            rows_left.append(row_left)
            rows_right.append(row_right)
            heads.append(head)
        upper.append(jnp.where(cols >= rows + SUB * p, here_left * scale, 0.0))
        inverse.append(here_right * scale)
        for g in range(p + 1, groups):
            columns = [lane(left[g], SUB * p + j) for j in range(SUB)]
            for j in range(SUB):
                factor = columns[j] * pivots[j]
                for l in range(j + 1, SUB):
                    columns[l] = columns[l] - factor * heads[j][l]
                left[g] = left[g] - factor * rows_left[j]
                right[g] = right[g] - factor * rows_right[j]
    return jnp.concatenate(upper, 0), jnp.concatenate(inverse, 0)


def head_row_kernel(index, *refs):
    raw_ref = refs[0]
    above = refs[1 : 1 + index]
    inverses = refs[1 + index : 1 + 2 * index]
    row_ref, inverse_ref, work = refs[1 + 2 * index :]
    here = slice(index * BLOCK, (index + 1) * BLOCK)
    diagonal = raw_ref[:, here]
    for b in range(index):
        block = raw_ref[:, b * BLOCK : (b + 1) * BLOCK]
        if b:
            block = block - exact(row_ref[:, : b * BLOCK], above[b][:, : b * BLOCK])
        row_ref[:, b * BLOCK : (b + 1) * BLOCK] = exact(block, inverses[b][...])
    if index:
        solved = row_ref[:, : index * BLOCK]
        diagonal = diagonal - exact(solved, solved)
    work[...] = diagonal
    row_ref[:, here] = jnp.zeros((BLOCK, BLOCK), jnp.float32)
    inverse_ref[...] = jnp.zeros((BLOCK, BLOCK), jnp.float32)
    start = index * BLOCK

    def step(i, carry):
        place = pl.ds(pl.multiple_of(i * LEAF, LEAF), LEAF)
        upper, inverse = leaf(work[place, place])
        row_ref[place, pl.ds(pl.multiple_of(start + i * LEAF, LEAF), LEAF)] = upper.T
        inverse_ref[place, place] = inverse

        @pl.when(i == 0)
        def _():
            below = exact(work[LEAF:, :LEAF], inverse)
            row_ref[LEAF:, start : start + LEAF] = below
            work[LEAF:, LEAF:] = work[LEAF:, LEAF:] - exact(below, below)
            work[LEAF:, :LEAF] = exact(below, inverse, NN)

        @pl.when(i == 1)
        def _():
            inverse_ref[LEAF:, :LEAF] = -exact(inverse, work[LEAF:, :LEAF], NN)

        return carry

    lax.fori_loop(0, BLOCK // LEAF, step, 0)


def head_row(index, raw, above, inverses):
    return pl.pallas_call(
        functools.partial(head_row_kernel, index),
        out_shape=[
            jax.ShapeDtypeStruct((BLOCK, (index + 1) * BLOCK), jnp.float32),
            jax.ShapeDtypeStruct((BLOCK, BLOCK), jnp.float32),
        ],
        scratch_shapes=[pltpu.VMEM((BLOCK, BLOCK), jnp.float32)],
        compiler_params=pltpu.CompilerParams(vmem_limit_bytes=24 * 2**20),
        cost_estimate=pl.CostEstimate(flops=10_000_000_000, bytes_accessed=2**20, transcendentals=0),
        name=f"head_row_{index}",
    )(raw, *above, *inverses)


def finish_kernel(first_slot, col_count, place_ref, own_ref, mirror_ref, slab_ref, *refs):
    factor_rows = refs[:HEAD_BLOCKS]
    inverses = refs[HEAD_BLOCKS : 2 * HEAD_BLOCKS]
    out_ref, high_ref, low_ref = refs[2 * HEAD_BLOCKS :]
    row_count, width = slab_ref.shape
    first_row_block = place_ref[0] * (row_count // BLOCK)
    col_index = place_ref[1]
    mirror_rows = mirror_ref.shape[0]
    row_splits = [split(factor_rows[b][:, : b * BLOCK]) if b else None for b in range(HEAD_BLOCKS)]
    inverse_splits = [split(inverses[b][...]) for b in range(HEAD_BLOCKS)]
    out_ref[...] = slab_ref[...]

    def solve(rows, source_ref, source_rows, row_block):
        for b in range(HEAD_BLOCKS):
            here = slice(b * BLOCK, (b + 1) * BLOCK)
            value = source_ref[source_rows, here]
            if b:
                done = slice(0, b * BLOCK)
                value = value - three((high_ref[rows, done], low_ref[rows, done]), row_splits[b])
            solved = three(split(value), inverse_splits[b])
            kept = solved
            if row_block is not None:
                in_factor = jnp.where(row_block == b, factor_rows[b][:, here], jnp.where(row_block < b, 0.0, solved))
                slot = b // col_count

                @pl.when(col_index == b % col_count)
                def _():
                    out_ref[source_rows, slot * BLOCK : (slot + 1) * BLOCK] = in_factor

            high, low = split(kept)
            high_ref[rows, here] = high
            low_ref[rows, here] = low

    def own_tile(i, carry):
        place = pl.ds(pl.multiple_of(i * BLOCK, BLOCK), BLOCK)
        solve(place, own_ref, place, first_row_block + i)
        return carry

    def mirror_tile(i, carry):
        place = pl.ds(pl.multiple_of(row_count + i * BLOCK, BLOCK), BLOCK)
        solve(place, mirror_ref, pl.ds(pl.multiple_of(i * BLOCK, BLOCK), BLOCK), None)
        return carry

    lax.fori_loop(0, row_count // BLOCK, own_tile, 0)
    lax.fori_loop(0, mirror_rows // BLOCK, mirror_tile, 0)
    panel = 2 * BLOCK
    for i in range(row_count // BLOCK):
        rows = slice(i * BLOCK, (i + 1) * BLOCK)
        for k in range(first_slot, width // BLOCK):
            other = slice(row_count + (k - first_slot) * BLOCK, row_count + (k - first_slot + 1) * BLOCK)
            here = slice(k * BLOCK, (k + 1) * BLOCK)
            trailing = k * col_count + col_index >= HEAD_BLOCKS
            for count in range(1, PANELS + 1):
                done = slice(0, count * panel)
                block = first_row_block + i
                reached = block >= 2 * count
                if count < PANELS:
                    reached = reached & (block < 2 * count + 2)

                @pl.when(reached & trailing)
                def _():
                    change = three((high_ref[rows, done], low_ref[rows, done]), (high_ref[other, done], low_ref[other, done]))
                    out_ref[rows, here] = slab_ref[rows, here] - change


def finish(first_slot, col_count, place, own, mirror, slab, factor_rows, inverses):
    vmem = pl.BlockSpec(memory_space=pltpu.VMEM)
    rows = own.shape[0] + mirror.shape[0]
    return pl.pallas_call(
        functools.partial(finish_kernel, first_slot, col_count),
        out_shape=jax.ShapeDtypeStruct(slab.shape, jnp.float32),
        in_specs=[pl.BlockSpec(memory_space=pltpu.SMEM)] + [vmem] * (3 + 2 * HEAD_BLOCKS),
        out_specs=vmem,
        scratch_shapes=[pltpu.VMEM((rows, HEAD), jnp.bfloat16)] * 2,
        compiler_params=pltpu.CompilerParams(vmem_limit_bytes=48 * 2**20),
        cost_estimate=pl.CostEstimate(flops=20_000_000_000, bytes_accessed=2**23, transcendentals=0),
        name="finish",
    )(place, own, mirror, slab, *factor_rows, *inverses)


def gathered(slab):
    row_count, width = slab.shape
    col_count = lax.axis_size("col")
    owners = min(col_count, HEAD_BLOCKS)
    slots = HEAD_BLOCKS // owners
    first_slot = HEAD_BLOCKS // col_count
    own = lax.all_gather(slab[:, : slots * BLOCK], "col")[:owners]
    own = own.reshape(owners, row_count, slots, BLOCK).transpose(1, 2, 0, 3).reshape(row_count, HEAD)
    head_devices = HEAD // row_count
    head = lax.all_gather(own, "row")[:head_devices].reshape(HEAD, HEAD)
    mirror = lax.all_gather(slab[:, first_slot * BLOCK :], "row")[:head_devices]
    mirror = mirror.reshape(HEAD, width - first_slot * BLOCK).T
    raw = [head[b * BLOCK : (b + 1) * BLOCK, : (b + 1) * BLOCK] for b in range(HEAD_BLOCKS)]
    return raw, own, mirror


def exchanged(slab):
    row_count, width = slab.shape
    col_count = lax.axis_size("col")
    cores = 2
    ys = col_count // cores
    xs = ys
    zs = lax.axis_size("row") // xs
    r, c = lax.axis_index("row"), lax.axis_index("col")
    z, x, y, core = r // xs, r % xs, c // cores, c % cores
    tile = slab[:, :BLOCK]

    def flat(z, x, y, core):
        return (z * xs + x) * col_count + y * cores + core

    def send(value, pairs):
        return lax.ppermute(value, ("row", "col"), [(flat(*a), flat(*b)) for a, b in pairs])

    def plane(level=None):
        return [(a, b) for a in range(xs) for b in range(ys)]

    everyone = [(k, a, b, e) for k in range(zs) for a, b in plane() for e in range(cores)]

    def swap_core(value):
        return send(value, [((k, a, b, e), (k, a, b, 1 - e)) for k, a, b, e in everyone])

    def down(value):
        copies = [send(value, [((0, a, b, e), (k, a, b, e)) for a, b in plane() for e in range(cores)]) for k in range(1, zs)]
        return jnp.where(z == 0, value, sum(copies[1:], copies[0]))

    def across(value):
        flips = {}
        for dx, dy in ((1, 0), (0, 1), (1, 1)):
            flips[dx, dy] = send(value, [((k, a, b, e), (k, a ^ dx, b ^ dy, e)) for k, a, b, e in everyone])
        flips[0, 0] = value
        found = {}
        for a, b in plane():
            at_x = [jnp.where(y == b, flips[dx, 0], flips[dx, 1]) for dx in (0, 1)]
            found[a, b] = jnp.where(x == a, at_x[0], at_x[1])
        return found

    half = BLOCK // 2
    lower = send(tile[BLOCK + half :], [((0, 0, 0, 0), (0, 0, 0, 1))])
    packed = jnp.where(
        core == 0,
        tile[: BLOCK + half],
        jnp.concatenate([tile[BLOCK:], lower], 0),
    )
    quarter = packed.shape[0] // (xs * ys)
    pieces = [packed[i * quarter : (i + 1) * quarter] for i in range(xs * ys)]
    mine = jnp.where((x == 0) & (y == 0), pieces[0], 0.0)
    for i, (a, b) in enumerate(plane()):
        if i:
            mine = mine + send(pieces[i], [((0, 0, 0, e), (0, a, b, e)) for e in range(cores)])
    first = across(down(mine))
    first = jnp.concatenate([first[spot] for spot in plane()], 0)
    second = swap_core(first)
    zero, one = jnp.where(core == 0, first, second), jnp.where(core == 0, second, first)
    raw = [zero[:BLOCK], jnp.concatenate([jnp.concatenate([zero[BLOCK:], one[BLOCK:]], 0), one[:BLOCK]], 1)]
    upper = send(tile[:BLOCK], [((0, 1, b, e), (0, 0, b, e)) for b in range(ys) for e in range(cores)])
    rest = across(down(jnp.where(x == 0, upper, tile[BLOCK:])))
    for a in range(xs):
        pair = jnp.concatenate([rest[a, b] for b in range(ys)], 0)
        other = swap_core(pair)
        even, odd = jnp.where(core == 0, pair, other), jnp.where(core == 0, other, pair)
        blocks = [block[b * BLOCK : (b + 1) * BLOCK] for b in range(ys) for block in (even, odd)]
        raw.append(jnp.concatenate(blocks[: 3 + a], 1))
    own = lax.all_gather(tile, "col")
    own = own.transpose(1, 0, 2).reshape(row_count, HEAD)
    turned = send(tile, [((k, a, 1 - a, e), (k, 1 - a, a, e)) for k in range(1, zs) for a in range(xs) for e in range(cores)])
    part = jnp.where(x == y, tile, turned)
    steps = zs - 1
    held = [part]
    for shift in range(1, steps):
        held.append(
            send(part, [((1 + k, a, b, e), (1 + (k + shift) % steps, a, b, e)) for k in range(steps) for a, b in plane() for e in range(cores)])
        )
    ordered = []
    for k in range(1, zs):
        chosen = held[0]
        for shift in range(1, steps):
            chosen = jnp.where((z - k) % steps == shift, held[shift], chosen)
        ordered.append(chosen)
    ordered = jnp.stack(ordered, 0)
    keep = jnp.where(core == 0, ordered[:, :BLOCK], ordered[:, BLOCK:])
    give = jnp.where(core == 0, ordered[:, BLOCK:], ordered[:, :BLOCK])
    got = swap_core(give)
    wide = jnp.where(core == 0, jnp.concatenate([keep, got], 2), jnp.concatenate([got, keep], 2))
    straight = slab[:, BLOCK:].T.reshape(steps, BLOCK, row_count)
    wide = jnp.where(z == 0, straight, wide)
    over = send(wide, [((k, a, b, e), (k, 1 - a, b, e)) for k, a, b, e in everyone])
    mirror = jnp.where(x == 0, jnp.concatenate([wide, over], 2), jnp.concatenate([over, wide], 2))
    return raw, own, mirror.reshape(steps * BLOCK, HEAD)


def shards(slab):
    row_count, width = slab.shape
    row_total, col_count = lax.axis_size("row"), lax.axis_size("col")
    slots = width // BLOCK
    fits = (
        row_count == 2 * BLOCK
        and col_count == HEAD_BLOCKS
        and slots > 1
        and row_total == (col_count // 2) * slots
    )
    raw, own, mirror = exchanged(slab) if fits else gathered(slab)
    factor_rows, inverses = [], []
    for b in range(HEAD_BLOCKS):
        row, inverse = head_row(b, raw[b], factor_rows, inverses)
        factor_rows.append(row)
        inverses.append(inverse)
    place = jnp.stack([lax.axis_index("row"), lax.axis_index("col")]).astype(jnp.int32)
    return finish(HEAD_BLOCKS // col_count, col_count, place, own, mirror, slab, factor_rows, inverses)


def solution(mesh):
    in_specs = (P("row", "col"),)
    out_specs = P("row", "col")
    return jax.shard_map(shards, mesh=mesh, in_specs=in_specs, out_specs=out_specs, check_vma=False)
```

time: 984 us -> 178 us (0.18); the launches traced: 971 us -> 178 us
  waiting for transfers between devices: 619 us -> 48.4 us
  other arithmetic: 241 us -> 13.1 us
  Pallas kernels: 0 us -> 65.7 us
  local copies, waits for them, and re-layouts: 50.6 us -> 10.6 us
  matrix products: 39.4 us -> 0 us
  starting transfers between devices: 0.76 us -> 25.9 us
    psum x10 -> x0, waiting for transfers between devices: 618 us -> none  [from_root(): return lax.psum(kept, axis)]
    another operation x39 -> x3, other arithmetic: 225 us -> 0.34 us  [the longest x2 0.26 us: exchanged(): ordered = jnp.stack(ordered, 0)]
    pallas_call x0 -> x5, Pallas kernels: none -> 65.7 us  [the longest x4 44.2 us: head_row(): pl.pallas_call(functools.partial(head_row_kernel, index), out_shape=[jax....]
    ppermute x0 -> x25, waiting for transfers between devices: none -> 48.4 us  [send(): lax.ppermute(value, ('row', 'col'), [(flat(*a), flat(*b)) for a, b in pai...]
    another operation x66 -> x0, local copies, waits for them, and re-layouts: 31.6 us -> none  [the longest x45 26 us: shards(): jax.scipy.linalg.solve_triangular(lower_factor, identity, lower=True)]
    ppermute x0 -> x25, starting transfers between devices: none -> 25.9 us  [send(): lax.ppermute(value, ('row', 'col'), [(flat(*a), flat(*b)) for a, b in pai...]
    dot_general x10 -> x0, matrix products: 21.3 us -> none  [the longest x2 12.1 us: shards(): change = jnp.einsum('rp,kcp->rkc', panel_left, mirrored, precision=PRECISE)]
    another operation x20 -> x0, matrix products: 18.2 us -> none  [the longest x12 9.58 us: shards(): jax.scipy.linalg.solve_triangular(lower_factor, identity, lower=True)]
  transfers between devices with their start and end apart: 10 -> 26, of which waited for: 10 -> 3; matrix products, arithmetic and copies ran while one was open for 1% -> 9% of each run, Pallas kernels for 0% -> 25%
where the time goes in v1:
time: 178 us
  Pallas kernels  65.7 us (37%)
  waiting for transfers between devices  48.4 us (27%)
  starting transfers between devices  25.9 us (15%)
  between operations  14 us (8%)
  other arithmetic  13.1 us (7%)
  local copies, waits for them, and re-layouts  10.6 us (6%)
    ppermute x25, waiting for transfers between devices, send(): lax.ppermute(value, ('row', 'col'), [(flat(*a), flat(*b)) for a, b in pai...  48.4 us
    pallas_call x4, Pallas kernels, head_row(): pl.pallas_call(functools.partial(head_row_kernel, index), out_shape=[jax....  44.2 us
    ppermute x25, starting transfers between devices, send(): lax.ppermute(value, ('row', 'col'), [(flat(*a), flat(*b)) for a, b in pai...  25.9 us
    pallas_call x1, Pallas kernels, finish(): pl.pallas_call(functools.partial(finish_kernel, first_slot, col_count), o...  21.5 us
    select_n x1, other arithmetic, exchanged(): jnp.where(x == 0, jnp.concatenate([wide, over], 2), jnp.concatenate([over...  4.38 us
    unnamed x14, local copies, waits for them, and re-layouts  4.29 us
  transfers between devices with their start and end apart: 26, of which 3 were waited for; matrix products, arithmetic and copies ran while one was open for 9% of the time, Pallas kernels for 25%

profile of v1, /device:TPU:14, one launch (start us, length us, event | category | flops | bytes accessed | tf_op | source)
XLA Modules:
  0.0 177.7 jit_solution(9726380230929071799)
XLA Ops:
  6.5 1.0 slice.91
  7.5 0.7 collective-permute-start.16
  8.2 0.9 slice.82
  9.8 1.1 broadcast_select_fusion.14
  11.0 1.0 maximum_select_fusion.3
  14.2 1.3 collective-permute-start.10
  15.5 1.3 collective-permute-start.11
  16.8 0.7 collective-permute-start
  17.6 1.3 collective-permute-start.17
  18.9 1.4 collective-permute-start.18
  20.3 1.4 collective-permute-start.19
  21.7 1.3 collective-permute-start.9
  23.1 1.3 slice.77
  24.3 3.1 %copy.4 = f32[512,768]{0,1:T(8,128)} copy(f32[512,768]{1,0:T(8,128)} %slice.77) | data formatting | bytes 3145728
  27.4 26.7 %collective-permute-done.9 = f32[96,256]{1,0:T(8,128)} collective-permute-done((f32[96,256]{1,0:T(8,128)S(1)}, f32[96,256]{1,0:T(8,128)}, u32[]{:S(2)}, u32[]{:S(2)}) %collective-permute-start.9) | collective-permute-done | bytes 98336 | tf_op jit(solution)/shard_map/ppermute | solution.py:251
  54.0 1.0 add_select_fusion.1
  55.3 3.4 %collective-permute-start.14 = (f32[96,256]{1,0:T(8,128)S(1)}, f32[96,256]{1,0:T(8,128)S(1)}, u32[]{:S(2)}, u32[]{:S(2)}) collective-permute-start(f32[96,256]{1,0:T(8,128)S(1)} %add_select_fusion.1), channel_id=1, source_target_pairs={{0,6},{1,7},{2,4},{3,5},{4,2},{5,3},{6,0},{7,1},{8,14},{9,15},{10,... | collective-permute-start | bytes 294920 | tf_op jit(solution)/shard_map/ppermute | solution.py:251
  58.6 1.2 add_select_fusion
  60.6 3.0 %collective-permute-start.22 = (f32[256,256]{1,0:T(8,128)S(1)}, f32[256,256]{1,0:T(8,128)S(1)}, u32[]{:S(2)}, u32[]{:S(2)}) collective-permute-start(f32[256,256]{1,0:T(8,128)S(1)} %add_select_fusion), channel_id=1, source_target_pairs={{0,6},{1,7},{2,4},{3,5},{4,2},{5,3},{6,0},{7,1},{8,14},{9,15},{10,... | collective-permute-start | bytes 786440 | tf_op jit(solution)/shard_map/ppermute | solution.py:251
  63.6 1.9 %collective-permute-start.1 = (f32[512,256]{1,0:T(8,128)S(1)}, f32[512,256]{1,0:T(8,128)S(1)}, u32[]{:S(2)}, u32[]{:S(2)}) collective-permute-start(f32[512,256]{1,0:T(8,128)S(1)} %broadcast_select_fusion.3), channel_id=1, source_target_pairs={{8,24},{9,25},{10,26},{11,27},{12,28},{13,29},{14,30},{15,31},{16,... | collective-permute-start | bytes 1572872 | tf_op jit(solution)/shard_map/ppermute | solution.py:251
  65.5 4.1 %collective-permute-start.2 = (f32[512,256]{1,0:T(8,128)S(1)}, f32[512,256]{1,0:T(8,128)S(1)}, u32[]{:S(2)}, u32[]{:S(2)}) collective-permute-start(f32[512,256]{1,0:T(8,128)S(1)} %broadcast_select_fusion.3), channel_id=1, source_target_pairs={{8,16},{9,17},{10,18},{11,19},{12,20},{13,21},{14,22},{15,23},{16,... | collective-permute-start | bytes 1572872 | tf_op jit(solution)/shard_map/ppermute | solution.py:251
  69.8 3.7 %collective-permute-done.22 = f32[256,256]{1,0:T(8,128)S(1)} collective-permute-done((f32[256,256]{1,0:T(8,128)S(1)}, f32[256,256]{1,0:T(8,128)S(1)}, u32[]{:S(2)}, u32[]{:S(2)}) %collective-permute-start.22) | collective-permute-done | bytes 262176 | tf_op jit(solution)/shard_map/ppermute | solution.py:251
  74.5 9.3 %head_row_0.1 = (f32[256,256]{1,0:T(8,128)S(1)}, f32[256,256]{1,0:T(8,128)S(1)}) custom-call(f32[256,256]{1,0:T(8,128)S(1)} %slice.105.refs_0_), custom_call_target="tpu_custom_call" | custom-call | flops 10000000000 | bytes 1048576 | tf_op jit(solution)/shard_map/head_row_0/pallas_call | solution.py:127
  83.8 10.3 %head_row_1.1 = (f32[256,512]{1,0:T(8,128)S(1)}, f32[256,256]{1,0:T(8,128)S(1)}) custom-call(f32[256,512]{1,0:T(8,128)S(1)} %pad_maximum_fusion.4.refs_0_, f32[256,256]{1,0:T(8,128)S(1)} %get-tuple-element.13.refs_1_.refs_0_, f32[256,256]{1,0:T(8,128)S(1)} %get-tuple-element.14.refs_2_.refs_3_.refs_4_), custom_call_target="tpu_custom_call" | custom-call | flops 10000000000 | bytes 1048576 | tf_op jit(solution)/shard_map/head_row_1/pallas_call | solution.py:127
  95.0 11.3 %head_row_2.1 = (f32[256,768]{1,0:T(8,128)S(1)}, f32[256,256]{1,0:T(8,128)S(1)}) custom-call(f32[256,768]{1,0:T(8,128)S(1)} %pad_maximum_fusion.2.refs_0_, f32[256,256]{1,0:T(8,128)S(1)} %get-tuple-element.13.refs_1_.refs_0_, f32[256,512]{1,0:T(8,128)S(1)} %get-tuple-element.15.refs_2_.refs_1_, f32[256,256]{1,0:T(8,128)S(1)} %get-tuple-element.14.refs_2_.refs_3_.refs_4_, ...), custom_call_target="tpu_custom_call" | custom-call | flops 10000000000 | bytes 1048576 | tf_op jit(solution)/shard_map/head_row_2/pallas_call | solution.py:127
  106.4 1.5 fusion.1
  108.1 13.3 %head_row_3.1 = (f32[256,1024]{1,0:T(8,128)S(1)}, f32[256,256]{1,0:T(8,128)S(1)}) custom-call(f32[256,1024]{1,0:T(8,128)S(1)} %pad_maximum_fusion.1.refs_0_, f32[256,256]{1,0:T(8,128)S(1)} %get-tuple-element.13.refs_1_.refs_0_, f32[256,512]{1,0:T(8,128)S(1)} %get-tuple-element.15.refs_2_.refs_1_, f32[256,768]{1,0:T(8,128)S(1)} %get-tuple-element.17.refs_3_.refs_2_, ...), custom_call_target="tpu_custom_call" | custom-call | flops 10000000000 | bytes 1048576 | tf_op jit(solution)/shard_map/head_row_3/pallas_call | solution.py:127
  122.1 1.5 fusion
  123.6 2.9 %copy.2 = f32[4,512,256]{2,0,1:T(4,128)S(1)} copy(f32[4,512,256]{2,1,0:T(8,128)} %bitcast.24) | data formatting | bytes 4194304 | tf_op jit(solution)/shard_map/all_gather | solution.py:302
  127.0 18.0 %collective-permute-done.4 = f32[3,256,512]{2,1,0:T(8,128)} collective-permute-done((f32[3,256,512]{2,1,0:T(8,128)}, f32[3,256,512]{2,1,0:T(8,128)}, u32[]{:S(2)}, u32[]{:S(2)}) %collective-permute-start.4) | collective-permute-done | bytes 1572896 | tf_op jit(solution)/shard_map/ppermute | solution.py:251
  145.0 4.4 %maximum_select_fusion.mirror_ref = f32[768,1024]{1,0:T(8,128)} fusion(f32[768,512]{1,0:T(8,128)} %bitcast.11, f32[768,512]{1,0:T(8,128)S(1)} %copy-done.4, pred[]{:T(512)S(6)} %eq.35), kind=kLoop, calls=%fused_computation | loop fusion | flops 2359296 | bytes 6291457 | tf_op jit(solution)/shard_map/jit(_where)/select_n | solution.py:326
  149.4 21.5 %finish.1 = f32[512,1024]{1,0:T(8,128)} custom-call(s32[2]{0:T(128)S(1)} %pad_add_fusion.place_ref, f32[512,1024]{1,0:T(8,128)S(1)} %bitcast.19, f32[768,1024]{1,0:T(8,128)} %maximum_select_fusion.mirror_ref, f32[512,1024]{1,0:T(8,128)} %slab_ref.1, f32[256,256]{1,0:T(8,128)S(1)} %get-tuple-element.13.refs_1_.refs_0_, ...), custom_call_target="tpu_custom_call" | custom-call | flops 20000000000 | bytes 8388608 | tf_op jit(solution)/shard_map/finish/pallas_call | solution.py:208
  (77 shorter events, 7.1 us)
Async XLA Ops:
  6.5 117.1 %all-gather.3.cloned.1.call-start = ((), (), s32[]{:S(2)}) async-start(), calls=%async_computation | async-start | bytes 2621440 | tf_op jit(solution)/shard_map/all_gather | solution.py:302
  7.5 2.3 %collective-permute-start.16 = (f32[256,256]{1,0:T(8,128)S(1)}, f32[256,256]{1,0:T(8,128)S(1)}, u32[]{:S(2)}, u32[]{:S(2)}) collective-permute-start(f32[256,256]{1,0:T(8,128)S(1)} %slice.91), channel_id=1, source_target_pairs={{4,0},{5,1},{6,2},{7,3}} | collective-permute-start | bytes 786440 | tf_op jit(solution)/shard_map/ppermute | solution.py:251
  9.1 1.9 %collective-permute-start.5 = (f32[128,256]{1,0:T(8,128)S(1)}, f32[128,256]{1,0:T(8,128)S(1)}, u32[]{:S(2)}, u32[]{:S(2)}) collective-permute-start(f32[128,256]{1,0:T(8,128)S(1)} %slice.82), channel_id=1, source_target_pairs={{0,1}} | collective-permute-start | bytes 393224 | tf_op jit(solution)/shard_map/ppermute | solution.py:251
  9.8 6.9 %copy-start.3 = (f32[512,1024]{1,0:T(8,128)S(1)}, f32[512,1024]{1,0:T(8,128)}, u32[]{:S(2)}) copy-start(f32[512,1024]{1,0:T(8,128)} %slab_ref.1) | copy-start | bytes 6291460
  12.1 2.0 %collective-permute-start.6 = (f32[96,256]{1,0:T(8,128)S(1)}, f32[96,256]{1,0:T(8,128)S(1)}, u32[]{:S(2)}, u32[]{:S(2)}) collective-permute-start(f32[96,256]{1,0:T(8,128)S(1)} %get-tuple-element.46), channel_id=1, source_target_pairs={{0,2},{1,3}} | collective-permute-start | bytes 294920 | tf_op jit(solution)/shard_map/ppermute | solution.py:251
  12.7 1.4 collective-permute-start.7
  13.4 0.7 collective-permute-start.8
  14.2 6.1 %collective-permute-start.10 = (f32[96,256]{1,0:T(8,128)S(1)}, f32[96,256]{1,0:T(8,128)}, u32[]{:S(2)}, u32[]{:S(2)}) collective-permute-start(f32[96,256]{1,0:T(8,128)S(1)} %fusion.6), channel_id=1, source_target_pairs={{0,16},{1,17},{2,18},{3,19},{4,20},{5,21},{6,22},{7,23}} | collective-permute-start | bytes 294920 | tf_op jit(solution)/shard_map/ppermute | solution.py:251
  15.5 6.2 %collective-permute-start.11 = (f32[96,256]{1,0:T(8,128)S(1)}, f32[96,256]{1,0:T(8,128)}, u32[]{:S(2)}, u32[]{:S(2)}) collective-permute-start(f32[96,256]{1,0:T(8,128)S(1)} %fusion.6), channel_id=1, source_target_pairs={{0,24},{1,25},{2,26},{3,27},{4,28},{5,29},{6,30},{7,31}} | collective-permute-start | bytes 294920 | tf_op jit(solution)/shard_map/ppermute | solution.py:251
  16.8 0.8 copy-start.5
  16.8 43.2 %collective-permute-start = (f32[512,256]{1,0:T(8,128)S(1)}, f32[512,256]{1,0:T(8,128)S(1)}, u32[]{:S(2)}, u32[]{:S(2)}) collective-permute-start(f32[512,256]{1,0:T(8,128)S(1)} %slice.76), channel_id=1, source_target_pairs={{10,12},{11,13},{12,10},{13,11},{18,20},{19,21},{20,18},{21,19},{2... | collective-permute-start | bytes 1572872 | tf_op jit(solution)/shard_map/ppermute | solution.py:251
  17.6 37.5 %collective-permute-start.17 = (f32[256,256]{1,0:T(8,128)S(1)}, f32[256,256]{1,0:T(8,128)}, u32[]{:S(2)}, u32[]{:S(2)}) collective-permute-start(f32[256,256]{1,0:T(8,128)S(1)} %get-tuple-element.21), channel_id=1, source_target_pairs={{0,8},{1,9},{2,10},{3,11},{4,12},{5,13},{6,14},{7,15}} | collective-permute-start | bytes 786440 | tf_op jit(solution)/shard_map/ppermute | solution.py:251
  18.9 36.3 %collective-permute-start.18 = (f32[256,256]{1,0:T(8,128)S(1)}, f32[256,256]{1,0:T(8,128)}, u32[]{:S(2)}, u32[]{:S(2)}) collective-permute-start(f32[256,256]{1,0:T(8,128)S(1)} %get-tuple-element.21), channel_id=1, source_target_pairs={{0,16},{1,17},{2,18},{3,19},{4,20},{5,21},{6,22},{7,23}} | collective-permute-start | bytes 786440 | tf_op jit(solution)/shard_map/ppermute | solution.py:251
  20.3 38.3 %collective-permute-start.19 = (f32[256,256]{1,0:T(8,128)S(1)}, f32[256,256]{1,0:T(8,128)}, u32[]{:S(2)}, u32[]{:S(2)}) collective-permute-start(f32[256,256]{1,0:T(8,128)S(1)} %get-tuple-element.21), channel_id=1, source_target_pairs={{0,24},{1,25},{2,26},{3,27},{4,28},{5,29},{6,30},{7,31}} | collective-permute-start | bytes 786440 | tf_op jit(solution)/shard_map/ppermute | solution.py:251
  21.7 32.4 %collective-permute-start.9 = (f32[96,256]{1,0:T(8,128)S(1)}, f32[96,256]{1,0:T(8,128)}, u32[]{:S(2)}, u32[]{:S(2)}) collective-permute-start(f32[96,256]{1,0:T(8,128)S(1)} %fusion.6), channel_id=1, source_target_pairs={{0,8},{1,9},{2,10},{3,11},{4,12},{5,13},{6,14},{7,15}} | collective-permute-start | bytes 294920 | tf_op jit(solution)/shard_map/ppermute | solution.py:251
  55.1 5.5 %collective-permute-start.12 = (f32[96,256]{1,0:T(8,128)S(1)}, f32[96,256]{1,0:T(8,128)S(1)}, u32[]{:S(2)}, u32[]{:S(2)}) collective-permute-start(f32[96,256]{1,0:T(8,128)S(1)} %add_select_fusion.1), channel_id=1, source_target_pairs={{0,2},{1,3},{2,0},{3,1},{4,6},{5,7},{6,4},{7,5},{8,10},{9,11},{10,... | collective-permute-start | bytes 294920 | tf_op jit(solution)/shard_map/ppermute | solution.py:251
  55.2 8.4 %collective-permute-start.13 = (f32[96,256]{1,0:T(8,128)S(1)}, f32[96,256]{1,0:T(8,128)S(1)}, u32[]{:S(2)}, u32[]{:S(2)}) collective-permute-start(f32[96,256]{1,0:T(8,128)S(1)} %add_select_fusion.1), channel_id=1, source_target_pairs={{0,4},{1,5},{2,6},{3,7},{4,0},{5,1},{6,2},{7,3},{8,12},{9,13},{10,... | collective-permute-start | bytes 294920 | tf_op jit(solution)/shard_map/ppermute | solution.py:251
  55.3 10.2 %collective-permute-start.14 = (f32[96,256]{1,0:T(8,128)S(1)}, f32[96,256]{1,0:T(8,128)S(1)}, u32[]{:S(2)}, u32[]{:S(2)}) collective-permute-start(f32[96,256]{1,0:T(8,128)S(1)} %add_select_fusion.1), channel_id=1, source_target_pairs={{0,6},{1,7},{2,4},{3,5},{4,2},{5,3},{6,0},{7,1},{8,14},{9,15},{10,... | collective-permute-start | bytes 294920 | tf_op jit(solution)/shard_map/ppermute | solution.py:251
  59.8 9.9 %collective-permute-start.20 = (f32[256,256]{1,0:T(8,128)S(1)}, f32[256,256]{1,0:T(8,128)S(1)}, u32[]{:S(2)}, u32[]{:S(2)}) collective-permute-start(f32[256,256]{1,0:T(8,128)S(1)} %add_select_fusion), channel_id=1, source_target_pairs={{0,2},{1,3},{2,0},{3,1},{4,6},{5,7},{6,4},{7,5},{8,10},{9,11},{10,... | collective-permute-start | bytes 786440 | tf_op jit(solution)/shard_map/ppermute | solution.py:251
  60.0 9.8 %collective-permute-start.21 = (f32[256,256]{1,0:T(8,128)S(1)}, f32[256,256]{1,0:T(8,128)S(1)}, u32[]{:S(2)}, u32[]{:S(2)}) collective-permute-start(f32[256,256]{1,0:T(8,128)S(1)} %add_select_fusion), channel_id=1, source_target_pairs={{0,4},{1,5},{2,6},{3,7},{4,0},{5,1},{6,2},{7,3},{8,12},{9,13},{10,... | collective-permute-start | bytes 786440 | tf_op jit(solution)/shard_map/ppermute | solution.py:251
  60.6 12.9 %collective-permute-start.22 = (f32[256,256]{1,0:T(8,128)S(1)}, f32[256,256]{1,0:T(8,128)S(1)}, u32[]{:S(2)}, u32[]{:S(2)}) collective-permute-start(f32[256,256]{1,0:T(8,128)S(1)} %add_select_fusion), channel_id=1, source_target_pairs={{0,6},{1,7},{2,4},{3,5},{4,2},{5,3},{6,0},{7,1},{8,14},{9,15},{10,... | collective-permute-start | bytes 786440 | tf_op jit(solution)/shard_map/ppermute | solution.py:251
  63.6 30.6 %collective-permute-start.1 = (f32[512,256]{1,0:T(8,128)S(1)}, f32[512,256]{1,0:T(8,128)S(1)}, u32[]{:S(2)}, u32[]{:S(2)}) collective-permute-start(f32[512,256]{1,0:T(8,128)S(1)} %broadcast_select_fusion.3), channel_id=1, source_target_pairs={{8,24},{9,25},{10,26},{11,27},{12,28},{13,29},{14,30},{15,31},{16,... | collective-permute-start | bytes 1572872 | tf_op jit(solution)/shard_map/ppermute | solution.py:251
  65.5 28.7 %collective-permute-start.2 = (f32[512,256]{1,0:T(8,128)S(1)}, f32[512,256]{1,0:T(8,128)S(1)}, u32[]{:S(2)}, u32[]{:S(2)}) collective-permute-start(f32[512,256]{1,0:T(8,128)S(1)} %broadcast_select_fusion.3), channel_id=1, source_target_pairs={{8,16},{9,17},{10,18},{11,19},{12,20},{13,21},{14,22},{15,23},{16,... | collective-permute-start | bytes 1572872 | tf_op jit(solution)/shard_map/ppermute | solution.py:251
  69.7 4.6 %collective-permute-start.15 = (f32[384,256]{1,0:T(8,128)S(1)}, f32[384,256]{1,0:T(8,128)S(1)}, u32[]{:S(2)}, u32[]{:S(2)}) collective-permute-start(f32[384,256]{1,0:T(8,128)S(1)} %pad_maximum_fusion.6), channel_id=1, source_target_pairs={{0,1},{1,0},{2,3},{3,2},{4,5},{5,4},{6,7},{7,6},{8,9},{9,8},{10,11... | collective-permute-start | bytes 1179656 | tf_op jit(solution)/shard_map/ppermute | solution.py:251
  73.6 21.0 %collective-permute-start.23 = (f32[512,256]{1,0:T(8,128)S(1)}, f32[512,256]{1,0:T(8,128)S(1)}, u32[]{:S(2)}, u32[]{:S(2)}) collective-permute-start(f32[512,256]{1,0:T(8,128)S(1)} %pad_maximum_fusion.3), channel_id=1, source_target_pairs={{0,1},{1,0},{2,3},{3,2},{4,5},{5,4},{6,7},{7,6},{8,9},{9,8},{10,11... | collective-permute-start | bytes 1572872 | tf_op jit(solution)/shard_map/ppermute | solution.py:251
  73.8 20.9 %collective-permute-start.24 = (f32[512,256]{1,0:T(8,128)S(1)}, f32[512,256]{1,0:T(8,128)S(1)}, u32[]{:S(2)}, u32[]{:S(2)}) collective-permute-start(f32[512,256]{1,0:T(8,128)S(1)} %pad_maximum_fusion.5), channel_id=1, source_target_pairs={{0,1},{1,0},{2,3},{3,2},{4,5},{5,4},{6,7},{7,6},{8,9},{9,8},{10,11... | collective-permute-start | bytes 1572872 | tf_op jit(solution)/shard_map/ppermute | solution.py:251
  94.6 11.8 %collective-permute-start.3 = (f32[3,256,256]{2,1,0:T(8,128)S(1)}, f32[3,256,256]{2,1,0:T(8,128)S(1)}, u32[]{:S(2)}, u32[]{:S(2)}) collective-permute-start(f32[3,256,256]{2,1,0:T(8,128)S(1)} %get-tuple-element.24), channel_id=1, source_target_pairs={{0,1},{1,0},{2,3},{3,2},{4,5},{5,4},{6,7},{7,6},{8,9},{9,8},{10,11... | collective-permute-start | bytes 2359304 | tf_op jit(solution)/shard_map/ppermute | solution.py:251
  95.0 11.3 %copy-start.2 = (f32[512,768]{0,1:T(8,128)S(1)}, f32[512,768]{0,1:T(8,128)}, u32[]{:S(2)}) copy-start(f32[512,768]{0,1:T(8,128)} %copy.4) | copy-start | bytes 4718596
  107.9 37.1 %collective-permute-start.4 = (f32[3,256,512]{2,1,0:T(8,128)}, f32[3,256,512]{2,1,0:T(8,128)}, u32[]{:S(2)}, u32[]{:S(2)}) collective-permute-start(f32[3,256,512]{2,1,0:T(8,128)} %fusion.1), channel_id=1, source_target_pairs={{0,4},{1,5},{2,6},{3,7},{4,0},{5,1},{6,2},{7,3},{8,12},{9,13},{10,... | collective-permute-start | bytes 4718600 | tf_op jit(solution)/shard_map/ppermute | solution.py:251
  121.4 0.7 copy-start
  126.5 18.5 %copy-start.4 = (f32[768,512]{1,0:T(8,128)S(1)}, f32[768,512]{1,0:T(8,128)}, u32[]{:S(2)}) copy-start(f32[768,512]{1,0:T(8,128)} %fusion) | copy-start | bytes 4718596
  145.0 4.4 %copy-start.1 = (f32[256,256]{1,0:T(8,128)S(1)}, f32[256,256]{1,0:T(8,128)}, u32[]{:S(2)}) copy-start(f32[256,256]{1,0:T(8,128)} %copy-done) | copy-start | bytes 786436
Sparse Core Ops, SparseCore 0:
  17.7 35.5 all-gather.2
